TPU v7x, 32 devices: a whole 2x2x4 slice. The times are simulated.
32 devices in a mesh: ens: 2 (over y), tile: 4 (over z), chan: 2 (over x), sec: 2 (over core).
Axes of the slice: x: 2, y: 2, z: 4, core: 2. Of those that a mesh axis runs over, the one named last changes fastest.
Arguments:
- ocean_state: bfloat16 [256, 128, 4, 128], P(('chan', 'sec'), ('ens', 'tile')), parts along dimension 1, may hold values from -6 to 6
- atmos: bfloat16 [16384, 384], P(('ens', 'tile')), parts along dimension 0, may hold values from -6 to 6
- flux_weight: bfloat16 [384, 256], P(None, ('chan', 'sec')), may hold values from -0.3125 to 0.3125
- conv_weight: bfloat16 [9, 256, 256], P(None, None, ('chan', 'sec')), may hold values from -0.125 to 0.125
- conv_bias: bfloat16 [256], P(('chan', 'sec')), may hold values from -3 to 3
- norm_gain: bfloat16 [256], P(('chan', 'sec')), may hold values from 0.5 to 2
- in_weight: bfloat16 [256, 1024], P(None, ('chan', 'sec')), may hold values from -0.375 to 0.375
- in_bias: bfloat16 [1024], P(('chan', 'sec')), may hold values from -3 to 3
- out_weight: bfloat16 [1024, 256], P(('chan', 'sec')), may hold values from -0.25 to 0.25
- layer_scale: bfloat16 [256], P(('chan', 'sec')), may hold values from 0.5 to 2
- cell_mask: int32 [64, 4, 128], P('tile'), may hold values from 0 to 1, as said below
- neighbours: int32 [64, 8], P('tile'), may hold values from -1 to 63, as said below
- remap: int32 [64, 4, 128], P('tile'), may hold values from 0 to 8191
Outputs:
- ocean_next: bfloat16 [256, 128, 4, 128], P(('chan', 'sec'), ('ens', 'tile')), parts along dimension 1
There are 2 independent parts, one for each index of `ens`. A program takes and returns all parts, laid end to end along the dimension named above; an argument that names none is the same for every part. Nothing has to cross between parts.
Inputs may be any that keep to these rules, and one draw needn't show every extreme that they name: `cell_mask`: land cells and every cell of a land block are 0. `neighbours`: for a slot among those of tile index t, each entry is -1 or a slot among those of tile indices t - 1, t and t + 1, i.e. in [(t - 1) * 16, (t + 2) * 16); entries that name land blocks are -1.
All inputs are finite; a program needn't handle non-finite values.
Results may differ from a plain program's by a relative error of at most 0.01.
Values may be sent and summed in bfloat16 or wider, within the bound.
A program may use at most 64 MiB of HBM per device.

v0:
```python
import jax
import jax.numpy as jnp
from jax import lax
from jax.sharding import PartitionSpec as P

norm_eps = 1e-06


def padded_2(cells, sides, width):
    for axis, dim in sides:
        count = lax.axis_size(axis)
        ends = count - 1
        head = lax.slice_in_dim(cells, 0, width, axis=dim)
        tail = lax.slice_in_dim(cells, cells.shape[dim] - width, cells.shape[dim], axis=dim)
        cells = jnp.concatenate(
            [
                lax.ppermute(tail, axis, [(i, (i + 1) % count) for i in range(ends)]),
                cells,
                lax.ppermute(head, axis, [((i + 1) % count, i) for i in range(ends)]),
            ],
            axis=dim,
        )
    return cells


def strips_of(state):
    return jnp.concatenate(
        [
            state[:, :, 0, :],
            state[:, :, -1, :],
            state[:, :, :, 0],
            state[:, :, :, -1],
            state[:, :, 0, 0:1],
            state[:, :, 0, -1:],
            state[:, :, -1, 0:1],
            state[:, :, -1, -1:],
        ],
        axis=2,
    )


def pad_blocks(state, strips, slot_index, valid):
    channels, slot_count, block_rows, block_cols = state.shape
    width = strips.shape[2]
    picked = jnp.take(strips, slot_index.reshape(-1), axis=1).reshape(
        channels, slot_count, 8, width
    )
    picked = jnp.where(valid[None, :, :, None], picked, jnp.zeros_like(picked))
    offset_base = 2 * block_cols + 2 * block_rows
    west_col = picked[:, :, 0, 2 * block_cols + block_rows : offset_base]
    east_col = picked[:, :, 1, 2 * block_cols : 2 * block_cols + block_rows]
    prev_row = picked[:, :, 2, block_cols : 2 * block_cols]
    next_row = picked[:, :, 3, 0:block_cols]
    top_row = jnp.concatenate(
        [
            picked[:, :, 4, offset_base + 3 : offset_base + 4],
            prev_row,
            picked[:, :, 5, offset_base + 2 : offset_base + 3],
        ],
        axis=2,
    )
    bottom_row = jnp.concatenate(
        [
            picked[:, :, 6, offset_base + 1 : offset_base + 2],
            next_row,
            picked[:, :, 7, offset_base : offset_base + 1],
        ],
        axis=2,
    )
    middle = jnp.concatenate([west_col[:, :, :, None], state, east_col[:, :, :, None]], axis=3)
    return jnp.concatenate([top_row[:, :, None, :], middle, bottom_row[:, :, None, :]], axis=2)


def conv_taps(padded, kernel, block_rows, block_cols):
    total = jnp.zeros((kernel.shape[2], padded.shape[1], block_rows, block_cols), jnp.float32)
    for tap in range(9):
        tap_row = tap // 3
        tap_col = tap % 3
        window = padded[:, :, tap_row : tap_row + block_rows, tap_col : tap_col + block_cols]
        total = total + jnp.einsum(
            "cskl,co->oskl", window, kernel[tap], preferred_element_type=jnp.float32
        )
    return total


def add_group(total, pair):
    term = jnp.einsum("hsij,hc->csij", pair[0], pair[1], preferred_element_type=jnp.float32).astype(
        jnp.bfloat16
    )
    term = lax.optimization_barrier(term)
    return (total + term.astype(jnp.float32), None)


def on_device(
    ocean_state,
    atmos,
    flux_weight,
    conv_weight,
    conv_bias,
    norm_gain,
    in_weight,
    in_bias,
    out_weight,
    layer_scale,
    cell_mask,
    neighbours,
    remap,
):
    chan_local, slot_count, block_rows, block_cols = ocean_state.shape
    groups = lax.axis_size(("chan", "sec"))
    channels = chan_local * groups
    hid_local = in_weight.shape[1]
    extended = padded_2(strips_of(ocean_state), (("tile", 1),), slot_count)
    first_slot = (lax.axis_index("tile") - 1) * slot_count
    valid = neighbours >= 0
    slot_index = jnp.clip(neighbours - first_slot, 0, 3 * slot_count - 1)
    padded = pad_blocks(ocean_state, extended, slot_index, valid)
    local_flux = jnp.einsum(
        "rf,fc->cr", atmos, flux_weight, preferred_element_type=jnp.float32
    ).astype(jnp.bfloat16)
    targets = remap.reshape(-1)
    piece = lax.all_gather(local_flux, "tile", axis=1, tiled=True)
    inside = (targets >= 0) & (targets < piece.shape[1])
    values = jnp.take(piece, jnp.clip(targets, 0, piece.shape[1] - 1), axis=1)
    forcing = jnp.where(inside[None, :], values, jnp.zeros_like(values))
    full_kernel, full_bias, full_gain, full_in, full_in_bias, full_out = (
        lax.all_gather(conv_weight, ("chan", "sec"), axis=2, tiled=True),
        lax.all_gather(conv_bias, ("chan", "sec"), axis=0, tiled=True),
        lax.all_gather(norm_gain, ("chan", "sec"), axis=0, tiled=True),
        lax.all_gather(in_weight, ("chan", "sec"), axis=1, tiled=True),
        lax.all_gather(in_bias, ("chan", "sec"), axis=0, tiled=True),
        lax.all_gather(out_weight, ("chan", "sec"), axis=0, tiled=True),
    )
    out_groups = full_out.reshape(groups, hid_local, channels)
    grouped = padded.reshape(
        chan_local, groups, slot_count // groups, block_rows + 2, block_cols + 2
    )
    tiles = lax.all_to_all(grouped, ("chan", "sec"), split_axis=1, concat_axis=0, tiled=True)[:, 0]
    conv_out = (
        conv_taps(tiles, full_kernel, block_rows, block_cols)
        + full_bias.astype(jnp.float32)[:, None, None, None]
    )
    squares = jnp.sum(conv_out * conv_out, axis=0)
    normed = (
        conv_out
        * lax.rsqrt(squares / channels + norm_eps)
        * full_gain.astype(jnp.float32)[:, None, None, None]
    ).astype(jnp.bfloat16)
    pre = jnp.einsum("csij,ch->hsij", normed, full_in, preferred_element_type=jnp.float32)
    hidden = jax.nn.gelu(
        pre + full_in_bias.astype(jnp.float32)[:, None, None, None], approximate=False
    ).astype(jnp.bfloat16)
    hid_groups = hidden.reshape((groups, hid_local) + hidden.shape[1:])
    summed, _ = lax.scan(
        add_group, jnp.zeros((channels,) + hidden.shape[1:], jnp.float32), (hid_groups, out_groups)
    )
    update = lax.all_to_all(
        summed[:, None], ("chan", "sec"), split_axis=0, concat_axis=1, tiled=True
    )
    update = update.reshape(chan_local, slot_count, block_rows, block_cols)
    total = (
        ocean_state.astype(jnp.float32)
        + layer_scale.astype(jnp.float32)[:, None, None, None] * update
    )
    total = total + forcing.reshape(chan_local, slot_count, block_rows, block_cols).astype(
        jnp.float32
    )
    return (cell_mask.astype(jnp.float32)[None] * total).astype(jnp.bfloat16)


def solution(mesh):
    placed = (
        P(("chan", "sec"), ("ens", "tile"), None, None),
        P(("ens", "tile"), None),
        P(None, ("chan", "sec")),
        P(None, None, ("chan", "sec")),
        P(("chan", "sec")),
        P(("chan", "sec")),
        P(None, ("chan", "sec")),
        P(("chan", "sec")),
        P(("chan", "sec"), None),
        P(("chan", "sec")),
        P("tile", None, None),
        P("tile", None),
        P("tile", None, None),
    )
    return jax.shard_map(
        on_device,
        mesh=mesh,
        in_specs=placed,
        out_specs=P(("chan", "sec"), ("ens", "tile"), None, None),
        check_vma=False,
    )
```

profile of v0, /device:TPU:0, one launch (start us, length us, event | category | flops | bytes accessed | tf_op | source)
XLA Modules:
  0.0 303.2 jit_solution(8548367868448448992)
XLA Ops:
  6.5 3.6 %fusion.51 = (bf16[64,16,1,128]{3,2,1,0:T(2,128)(2,1)S(1)}, bf16[64,16,1,128]{3,2,1,0:T(2,128)(2,1)}) fusion(bf16[64,16,4,128]{3,2,1,0:T(4,128)(2,1)} %param.15), kind=kLoop, calls=%fused_computation.95 | loop fusion | bytes 1048576 | tf_op jit(solution)/shard_map/slice | solution.py:30
  24.3 7.2 %copy.136 = bf16[64,16,4,1]{2,0,1,3:T(8,128)(2,1)S(1)} copy(bf16[64,16,4,1]{3,2,1,0:T(4,128)(2,1)} %get-tuple-element.80) | data formatting | bytes 16384 | tf_op jit(solution)/shard_map/squeeze | solution.py:31
  31.6 7.9 %copy.137 = bf16[64,16,4,1]{2,0,1,3:T(8,128)(2,1)} copy(bf16[64,16,4,1]{3,2,1,0:T(4,128)(2,1)} %get-tuple-element.79) | data formatting | bytes 16384 | tf_op jit(solution)/shard_map/squeeze | solution.py:32
  41.6 3.6 %concatenate.40 = bf16[64,16,268]{2,0,1:T(8,128)(2,1)} concatenate(bf16[64,16,128]{2,0,1:T(8,128)(2,1)} %get-tuple-element.89, bf16[64,16,128]{2,0,1:T(8,128)(2,1)} %get-tuple-element.88, bf16[64,16,4]{2,0,1:T(8,128)(2,1)S(1)} %bitcast.225, bf16[64,16,4]{2,0,1:T(8,128)(2,1)} %bitcast.226, bf16[64,16,1]{2,0,1:T(8,128)(2,1)} %copy.73, bf16[64,16,1]{2,0,1:T(8,128)(2,1)} %copy.74, ...), dimensions={2} | concatenate | bytes 1097728 | tf_op jit(solution)/shard_map/concatenate | solution.py:27
  45.3 5.8 %collective-permute-start = (bf16[64,16,268]{2,0,1:T(8,128)(2,1)}, bf16[64,16,268]{2,0,1:T(8,128)(2,1)}, u32[]{:S(2)}, u32[]{:S(2)}) collective-permute-start(bf16[64,16,268]{2,0,1:T(8,128)(2,1)} %concatenate.40), channel_id=1, source_target_pairs={{0,4},{4,8},{8,12},{1,5},{5,9},{9,13},{2,6},{6,10},{10,14},{3,7},{... | collective-permute-start | bytes 1646600 | tf_op jit(solution)/shard_map/ppermute | solution.py:17
  54.4 12.9 %collective-permute-done = bf16[64,16,268]{2,0,1:T(8,128)(2,1)} collective-permute-done((bf16[64,16,268]{2,0,1:T(8,128)(2,1)}, bf16[64,16,268]{2,0,1:T(8,128)(2,1)}, u32[]{:S(2)}, u32[]{:S(2)}) %collective-permute-start) | collective-permute-done | bytes 548896 | tf_op jit(solution)/shard_map/ppermute | solution.py:17
  67.3 5.0 %collective-permute-done.1 = bf16[64,16,268]{2,0,1:T(8,128)(2,1)} collective-permute-done((bf16[64,16,268]{2,0,1:T(8,128)(2,1)}, bf16[64,16,268]{2,0,1:T(8,128)(2,1)}, u32[]{:S(2)}, u32[]{:S(2)}) %collective-permute-start.1) | collective-permute-done | bytes 548896 | tf_op jit(solution)/shard_map/ppermute | solution.py:19
  75.8 5.8 %gather_fusion = bf16[128,64,268]{2,1,0:T(8,128)(2,1)} fusion(bf16[64,48,268]{2,0,1:T(8,128)(2,1)} %pad_maximum_fusion.1, s32[1024]{0:T(1024)S(1)} %pad_clamp_fusion), kind=kCustom, calls=%fused_computation | custom fusion | bytes 8782336 | tf_op jit(solution)/shard_map/jit(_take)/gather | solution.py:45
  81.5 13.8 %copy.78 = bf16[64,16,8,268]{0,1,3,2:T(8,128)(2,1)} copy(bf16[64,16,8,268]{3,0,2,1:T(8,128)(2,1)} %bitcast.217) | data formatting | bytes 8781824 | tf_op jit(solution)/shard_map/jit(_take)/gather | solution.py:45
  95.3 7.9 %select_select_fusion = bf16[64,16,8,268]{0,1,3,2:T(8,128)(2,1)} fusion(bf16[64,16,8,268]{0,1,3,2:T(8,128)(2,1)} %copy.78, pred[16,8]{0,1:T(8,128)(4,1)S(1)} %get-tuple-element.65, pred[16,8]{0,1:T(8,128)(4,1)S(1)} %get-tuple-element.85), kind=kLoop, calls=%fused_computation.10 | loop fusion | flops 4390912 | bytes 8782080 | tf_op jit(solution)/shard_map/jit(_where)/select_n | solution.py:48
  120.3 4.8 %all-to-all-start = ((bf16[64,4,4,6,130]{4,0,3,2,1:T(8,128)(2,1)}), bf16[64,4,4,6,130]{4,0,3,2,1:T(8,128)(2,1)}, u32[]{:S(2)}, u32[]{:S(2)}) async-start(bf16[64,4,4,6,130]{4,0,3,2,1:T(8,128)(2,1)} %pad_maximum_fusion), calls=%async_computation | async-start | bytes 6291456 | tf_op jit(solution)/shard_map/all_to_all | solution.py:138
  128.3 35.2 %all-reduce.2 = (bf16[256]{0:T(256)(128)(2,1)S(1)}, bf16[256]{0:T(256)(128)(2,1)S(1)}) all-reduce(bf16[256]{0:T(256)(128)(2,1)S(1)} %dynamic-update-slice, bf16[256]{0:T(256)(128)(2,1)S(1)} %dynamic-update-slice.1), channel_id=1, replica_groups=mesh['ens'=2,'tile'=4,'chan'=2,'sec'=2] {'chan','sec'}, use_global_device_ids=true, to_apply=%add | all-reduce | flops 512 | bytes 2048
  163.5 5.1 %all-gather = bf16[4,1,256]{2,1,0:T(2,128)(2,1)S(1)} all-gather(bf16[1,1,256]{2,1,0:T(2,128)(2,1)S(1)} %reshape.159), channel_id=1, replica_groups=mesh['ens'=2,'tile'=4,'chan'=2,'sec'=2] {'chan','sec'}, dimensions={0}, use_global_device_ids=true | all-gather | bytes 2560 | tf_op jit(solution)/shard_map/all_gather | solution.py:131
  168.6 7.3 %all_gather.25 = bf16[256,1024]{1,0:T(8,128)(2,1)S(1)} all-gather(bf16[256,256]{1,0:T(8,128)(2,1)S(1)} %copy-done.10), channel_id=1, replica_groups=mesh['ens'=2,'tile'=4,'chan'=2,'sec'=2] {'chan','sec'}, dimensions={1}, use_global_device_ids=true | all-gather | bytes 655360 | tf_op jit(solution)/shard_map/all_gather | solution.py:130
  176.0 7.9 %all_gather.21 = bf16[1024,256]{1,0:T(8,128)(2,1)} all-gather(bf16[256,256]{1,0:T(8,128)(2,1)S(1)} %copy-done.11), channel_id=1, replica_groups=mesh['ens'=2,'tile'=4,'chan'=2,'sec'=2] {'chan','sec'}, dimensions={0}, use_global_device_ids=true | all-gather | bytes 655360 | tf_op jit(solution)/shard_map/all_gather | solution.py:132
  184.0 7.3 %copy.90 = bf16[4,64,1,4,6,130]{1,0,5,4,3,2:T(4,128)(2,1)} copy(bf16[4,64,1,4,6,130]{5,1,4,3,0,2:T(8,128)(2,1)} %bitcast.24) | data formatting | bytes 3194880 | tf_op jit(solution)/shard_map/all_to_all | solution.py:138
  191.3 5.1 %squeeze.76 = bf16[256,4,6,130]{0,3,2,1:T(8,128)(2,1)} reshape(bf16[4,64,1,4,6,130]{1,0,5,4,3,2:T(4,128)(2,1)} %copy.90) | data formatting | bytes 3194880 | tf_op jit(solution)/shard_map/squeeze | solution.py:138
  203.1 20.7 %fusion.7 = bf16[1024,4,4,128]{0,3,2,1:T(8,128)(2,1)} fusion(f32[1024]{0:T(1024)S(1)} %bitcast.239, f32[4,4,128,256]{3,2,1,0:T(8,128)S(1)} %get-tuple-element.87, f32[256]{0:T(256)S(1)} %convert_element_type.43, f32[4,4,128]{2,1,0:T(4,128)S(1)} %add_rsqrt_fusion, bf16[256,1024]{1,0:T(8,128)(2,1)S(1)} %all_gather.25), kind=kOutput, calls=%fused_computation.13 | convolution fusion | flops 1213726720 | bytes 6829056 | tf_op jit(solution)/shard_map/csij,ch->hsij/dot_general | solution.py:149
  223.9 7.9 %reshape.135 = bf16[4,256,4,4,128]{1,0,4,3,2:T(4,128)(2,1)} reshape(bf16[1024,4,4,128]{0,3,2,1:T(8,128)(2,1)} %fusion.7) | data formatting | bytes 8388608 | tf_op jit(solution)/shard_map/reshape | solution.py:153
  231.8 7.5 %copy.101 = bf16[4,256,4,4,128]{4,1,3,2,0:T(8,128)(2,1)} copy(bf16[4,256,4,4,128]{1,0,4,3,2:T(4,128)(2,1)} %reshape.135) | data formatting | bytes 8388608
  239.3 9.9 %while.11 = (s32[]{:T(128)}, f32[256,4,4,128]{3,0,2,1:T(8,128)S(1)}, bf16[4,256,256]{2,1,0:T(8,128)(2,1)}, bf16[4,256,4,4,128]{4,1,3,2,0:T(8,128)(2,1)}, s32[]{:T(128)}, /*index=5*/s32[]{:T(128)}) while((s32[]{:T(128)}, f32[256,4,4,128]{3,0,2,1:T(8,128)S(1)}, bf16[4,256,256]{2,1,0:T(8,128)(2,1)}, ...), condition=%wide.region_2.3_spmd.clone, body=%wide.region_1.2_spmd.clone.sunk | while | flops 270532608 | bytes 7472207 | solution.py:154
  251.8 4.7 %all-to-all-start.1 = ((f32[256,1,4,4,128]{4,3,2,1,0:T(4,128)}), f32[256,1,4,4,128]{4,3,2,1,0:T(4,128)}, u32[]{:S(2)}, u32[]{:S(2)}) async-start(f32[256,1,4,4,128]{4,3,2,1,0:T(4,128)} %bitcast.218), calls=%async_computation.1 | async-start | bytes 4194304 | tf_op jit(solution)/shard_map/all_to_all | solution.py:157
  258.7 29.2 %gather_fusion.1 = bf16[8192,64]{1,0:T(8,128)(2,1)} fusion(bf16[64,8192]{0,1:T(8,128)(2,1)S(1)} %copy.104, s32[8192]{0:T(1024)S(1)} %broadcast_clamp_fusion), kind=kCustom, calls=%fused_computation.1 | custom fusion | bytes 2129920 | tf_op jit(solution)/shard_map/jit(_take)/gather | solution.py:124
  287.9 3.7 %copy.105 = bf16[64,16,4,128]{3,2,1,0:T(4,128)(2,1)} copy(bf16[64,16,4,128]{0,3,2,1:T(8,128)(2,1)} %bitcast.220) | data formatting | bytes 2097152 | tf_op jit(solution)/shard_map/jit(_take)/gather | solution.py:124
  (122 shorter events, 68.7 us)
Async XLA Ops:
  6.5 118.6 %copy-start = (bf16[2048,384]{1,0:T(8,128)(2,1)S(1)}, bf16[2048,384]{1,0:T(8,128)(2,1)}, u32[]{:S(2)}) copy-start(bf16[2048,384]{1,0:T(8,128)(2,1)} %param.16) | copy-start | bytes 4718596
  6.5 3.6 %copy-start.3 = (bf16[64,16,4,128]{3,2,1,0:T(4,128)(2,1)S(1)}, bf16[64,16,4,128]{3,2,1,0:T(4,128)(2,1)}, u32[]{:S(2)}) copy-start(bf16[64,16,4,128]{3,2,1,0:T(4,128)(2,1)} %param.15) | copy-start | bytes 3145732
  6.5 189.8 %all-gather.4.cloned.1.call-start = ((), (), s32[]{:S(2)}) async-start(), calls=%async_computation.2 | async-start | bytes 1474560 | tf_op jit(solution)/shard_map/all_gather | solution.py:127
  39.5 14.8 %copy-start.15 = (s32[16,8]{0,1:T(8,128)S(1)}, s32[16,8]{0,1:T(8,128)}, u32[]{:S(2)}) copy-start(s32[16,8]{0,1:T(8,128)} %param.26) | copy-start | bytes 1540
  45.3 22.0 %collective-permute-start = (bf16[64,16,268]{2,0,1:T(8,128)(2,1)}, bf16[64,16,268]{2,0,1:T(8,128)(2,1)}, u32[]{:S(2)}, u32[]{:S(2)}) collective-permute-start(bf16[64,16,268]{2,0,1:T(8,128)(2,1)} %concatenate.40), channel_id=1, source_target_pairs={{0,4},{4,8},{8,12},{1,5},{5,9},{9,13},{2,6},{6,10},{10,14},{3,7},{... | collective-permute-start | bytes 1646600 | tf_op jit(solution)/shard_map/ppermute | solution.py:17
  51.1 21.2 %collective-permute-start.1 = (bf16[64,16,268]{2,0,1:T(8,128)(2,1)}, bf16[64,16,268]{2,0,1:T(8,128)(2,1)}, u32[]{:S(2)}, u32[]{:S(2)}) collective-permute-start(bf16[64,16,268]{2,0,1:T(8,128)(2,1)} %concatenate.40), channel_id=1, source_target_pairs={{4,0},{8,4},{12,8},{5,1},{9,5},{13,9},{6,2},{10,6},{14,10},{7,3},{... | collective-permute-start | bytes 1646600 | tf_op jit(solution)/shard_map/ppermute | solution.py:19
  107.6 9.6 %copy-start.5 = (bf16[64,16,4,128]{3,0,2,1:T(8,128)(2,1)S(1)}, bf16[64,16,4,128]{3,0,2,1:T(8,128)(2,1)}, u32[]{:S(2)}) copy-start(bf16[64,16,4,128]{3,0,2,1:T(8,128)(2,1)} %copy.82) | copy-start | bytes 3145732
  114.2 2.9 copy-start.6
  114.2 2.9 copy-start.7
  120.2 4.9 %copy-start.13 = (bf16[384,64]{0,1:T(8,128)(2,1)S(1)}, bf16[384,64]{0,1:T(8,128)(2,1)}, u32[]{:S(2)}) copy-start(bf16[384,64]{0,1:T(8,128)(2,1)} %param.17) | copy-start | bytes 147460
  120.2 6.3 %copy-start.20 = (u32[32]{0:T(128)S(1)}, u32[32]{0:T(128)}, u32[]{:S(2)}) copy-start(u32[32]{0:T(128)} %constant.127) | copy-start | bytes 388
  120.2 7.6 %copy-start.16 = (bf16[64]{0:T(256)(128)(2,1)S(1)}, bf16[64]{0:T(256)(128)(2,1)}, u32[]{:S(2)}) copy-start(bf16[64]{0:T(256)(128)(2,1)} %param.19) | copy-start | bytes 388
  120.2 7.8 %copy-start.17 = (bf16[64]{0:T(256)(128)(2,1)S(1)}, bf16[64]{0:T(256)(128)(2,1)}, u32[]{:S(2)}) copy-start(bf16[64]{0:T(256)(128)(2,1)} %param.20) | copy-start | bytes 388
  120.2 43.3 %copy-start.18 = (bf16[256]{0:T(256)(128)(2,1)S(1)}, bf16[256]{0:T(256)(128)(2,1)}, u32[]{:S(2)}) copy-start(bf16[256]{0:T(256)(128)(2,1)} %param.22) | copy-start | bytes 1540
  120.2 48.4 %copy-start.14 = (s32[16,4,128]{2,1,0:T(4,128)S(1)}, s32[16,4,128]{2,1,0:T(4,128)}, u32[]{:S(2)}) copy-start(s32[16,4,128]{2,1,0:T(4,128)} %param.25) | copy-start | bytes 98308
  120.2 48.4 %copy-start.19 = (bf16[64]{0:T(256)(128)(2,1)S(1)}, bf16[64]{0:T(256)(128)(2,1)}, u32[]{:S(2)}) copy-start(bf16[64]{0:T(256)(128)(2,1)} %param.24) | copy-start | bytes 388
  120.3 48.4 %copy-start.10 = (bf16[256,256]{1,0:T(8,128)(2,1)S(1)}, bf16[256,256]{1,0:T(8,128)(2,1)}, u32[]{:S(2)}) copy-start(bf16[256,256]{1,0:T(8,128)(2,1)} %param.21) | copy-start | bytes 393220
  120.3 55.7 %copy-start.11 = (bf16[256,256]{1,0:T(8,128)(2,1)S(1)}, bf16[256,256]{1,0:T(8,128)(2,1)}, u32[]{:S(2)}) copy-start(bf16[256,256]{1,0:T(8,128)(2,1)} %param.23) | copy-start | bytes 393220
  120.3 63.7 %all-to-all-start = ((bf16[64,4,4,6,130]{4,0,3,2,1:T(8,128)(2,1)}), bf16[64,4,4,6,130]{4,0,3,2,1:T(8,128)(2,1)}, u32[]{:S(2)}, u32[]{:S(2)}) async-start(bf16[64,4,4,6,130]{4,0,3,2,1:T(8,128)(2,1)} %pad_maximum_fusion), calls=%async_computation | async-start | bytes 6291456 | tf_op jit(solution)/shard_map/all_to_all | solution.py:138
  125.1 58.9 %copy-start.12 = (s32[16,4,128]{2,1,0:T(4,128)S(1)}, s32[16,4,128]{2,1,0:T(4,128)}, u32[]{:S(2)}) copy-start(s32[16,4,128]{2,1,0:T(4,128)} %param.27) | copy-start | bytes 98308
  125.1 131.5 %all-gather.6.cloned.1.call-start = ((), (), s32[]{:S(2)}) async-start(), calls=%async_computation.3 | async-start | bytes 1310720 | tf_op jit(solution)/shard_map/all_gather | solution.py:122
  251.8 39.8 %all-to-all-start.1 = ((f32[256,1,4,4,128]{4,3,2,1,0:T(4,128)}), f32[256,1,4,4,128]{4,3,2,1,0:T(4,128)}, u32[]{:S(2)}, u32[]{:S(2)}) async-start(f32[256,1,4,4,128]{4,3,2,1,0:T(4,128)} %bitcast.218), calls=%async_computation.1 | async-start | bytes 4194304 | tf_op jit(solution)/shard_map/all_to_all | solution.py:157
  287.9 6.1 %copy-start.4 = (bf16[64,16,4,128]{3,2,1,0:T(4,128)(2,1)S(1)}, bf16[64,16,4,128]{3,2,1,0:T(4,128)(2,1)}, u32[]{:S(2)}) copy-start(bf16[64,16,4,128]{3,2,1,0:T(4,128)(2,1)} %param.15) | copy-start | bytes 3145732
  291.6 4.7 %copy-start.1 = (bf16[2048,384]{1,0:T(8,128)(2,1)S(1)}, bf16[2048,384]{1,0:T(8,128)(2,1)}, u32[]{:S(2)}) copy-start(bf16[2048,384]{1,0:T(8,128)(2,1)} %param.16) | copy-start | bytes 4718596
  (3 other events, 6.3 us)
Sparse Core Ops, SparseCore 0:
  52.7 19.5 all-gather.3
  127.5 27.7 all-gather.5
where the time goes:
time: 305 us; the launch traced here: 303 us
  local copies, waits for them, and re-layouts  140 us (46%)
  blocking collectives  55.6 us (18%)
  matrix products  35.6 us (12%)
  other arithmetic  22.6 us (7%)
  waiting for transfers between devices  17.9 us (6%)
  starting transfers between devices  16.8 us (6%)
  between operations  14.4 us (5%)
    unnamed x1, blocking collectives  35.2 us
    gather x2, local copies, waits for them, and re-layouts, on_device(): values = jnp.take(piece, jnp.clip(targets, 0, piece.shape[1] - 1), axis=1)  33 us
    dot_general x1, matrix products, on_device(): jnp.einsum('csij,ch->hsij', normed, full_in, preferred_element_type=jnp.f...  20.7 us
    gather x2, local copies, waits for them, and re-layouts, pad_blocks(): jnp.take(strips, slot_index.reshape(-1), axis=1)  19.6 us
    unnamed x54, local copies, waits for them, and re-layouts  15.9 us
    ppermute x1, waiting for transfers between devices, padded_2(): lax.ppermute(tail, axis, [(i, (i + 1) % count) for i in range(ends)])  12.9 us
    all_gather x1, blocking collectives, on_device(): lax.all_gather(out_weight, ('chan', 'sec'), axis=0, tiled=True)  7.95 us
    select_n x1, other arithmetic, pad_blocks(): picked = jnp.where(valid[None, :, :, None], picked, jnp.zeros_like(picked))  7.94 us
  transfers between devices with their start and end apart: 6, of which 2 were waited for; matrix products, arithmetic and copies ran while one was open for 51% of the time, Pallas kernels for 0%

commit v1 on v0

--- a/solution.py
+++ b/solution.py
@@ -154,9 +154,18 @@
     summed, _ = lax.scan(
         add_group, jnp.zeros((channels,) + hidden.shape[1:], jnp.float32), (hid_groups, out_groups)
     )
-    update = lax.all_to_all(
-        summed[:, None], ("chan", "sec"), split_axis=0, concat_axis=1, tiled=True
-    )
+    shard = summed[:, None]
+    ways, here = (lax.axis_size(("chan", "sec")), lax.axis_index(("chan", "sec")))
+    width_2 = shard.shape[0] // ways
+    turned = jnp.roll(shard, -here * width_2, axis=0)
+    got = [lax.slice_in_dim(turned, 0, width_2, axis=0)]
+    for far in range(1, ways):
+        sent = lax.slice_in_dim(turned, far * width_2, (far + 1) * width_2, axis=0)
+        got.append(
+            lax.ppermute(sent, ("chan", "sec"), [(d, (d + far) % ways) for d in range(ways)])
+        )
+    line = jnp.concatenate(got[::-1], axis=1)
+    update = jnp.roll(line, (here + 1) * got[0].shape[1], axis=1)
     update = update.reshape(chan_local, slot_count, block_rows, block_cols)
     total = (
         ocean_state.astype(jnp.float32)

time: 305 us -> 316 us (1.036)
  local copies, waits for them, and re-layouts: 140 us -> 150 us
    unnamed x54 -> x59, local copies, waits for them, and re-layouts: 15.9 us -> 23.5 us
    all_to_all x1 -> x0, starting transfers between devices: 4.7 us -> none  [on_device(): lax.all_to_all(summed[:, None], ('chan', 'sec'), split_axis=0, concat_axi...]
  transfers between devices with their start and end apart: 6 -> 8, of which waited for: 2 -> 2; matrix products, arithmetic and copies ran while one was open for 51% -> 51% of each run, Pallas kernels for 0% -> 0%
where the time goes in v1:
time: 316 us; the launch traced here: 313 us
  local copies, waits for them, and re-layouts  150 us (47%)
  blocking collectives  55.6 us (18%)
  matrix products  36.9 us (12%)
  other arithmetic  23.8 us (8%)
  waiting for transfers between devices  17.7 us (6%)
  between operations  14.6 us (5%)
  starting transfers between devices  14.1 us (4%)
    unnamed x1, blocking collectives  35.2 us
    gather x2, local copies, waits for them, and re-layouts, on_device(): values = jnp.take(piece, jnp.clip(targets, 0, piece.shape[1] - 1), axis=1)  32.7 us
    unnamed x59, local copies, waits for them, and re-layouts  23.5 us
    dot_general x1, matrix products, on_device(): jnp.einsum('csij,ch->hsij', normed, full_in, preferred_element_type=jnp.f...  20.8 us
    gather x2, local copies, waits for them, and re-layouts, pad_blocks(): jnp.take(strips, slot_index.reshape(-1), axis=1)  19.5 us
    ppermute x1, waiting for transfers between devices, padded_2(): lax.ppermute(tail, axis, [(i, (i + 1) % count) for i in range(ends)])  12.5 us
    all_gather x1, blocking collectives, on_device(): lax.all_gather(out_weight, ('chan', 'sec'), axis=0, tiled=True)  7.95 us
    select_n x1, other arithmetic, pad_blocks(): picked = jnp.where(valid[None, :, :, None], picked, jnp.zeros_like(picked))  7.94 us
  transfers between devices with their start and end apart: 8, of which 2 were waited for; matrix products, arithmetic and copies ran while one was open for 51% of the time, Pallas kernels for 0%

profile of v1, /device:TPU:0, one launch (start us, length us, event | category | flops | bytes accessed | tf_op | source)
XLA Modules:
  0.0 313.1 jit_solution(11479914184458584081)
XLA Ops:
  6.5 3.6 %fusion.53 = (bf16[64,16,1,128]{3,2,1,0:T(2,128)(2,1)S(1)}, bf16[64,16,1,128]{3,2,1,0:T(2,128)(2,1)}) fusion(bf16[64,16,4,128]{3,2,1,0:T(4,128)(2,1)} %param.15), kind=kLoop, calls=%fused_computation.107 | loop fusion | bytes 1048576 | tf_op jit(solution)/shard_map/slice | solution.py:30
  10.2 5.7 %fusion.51 = (bf16[64,16,1,1]{3,2,1,0:T(2,128)(2,1)}, bf16[64,16,1,1]{3,2,1,0:T(2,128)(2,1)}, bf16[64,16,1,1]{3,2,1,0:T(2,128)(2,1)}, bf16[64,16,1,1]{3,2,1,0:T(2,128)(2,1)}) fusion(bf16[64,16,4,128]{3,2,1,0:T(4,128)(2,1)} %param.15), kind=kLoop, calls=%fused_computation.105 | loop fusion | bytes 16384 | tf_op jit(solution)/shard_map/slice | solution.py:36
  27.0 7.9 %copy.135 = bf16[64,16,4,1]{2,0,1,3:T(8,128)(2,1)} copy(bf16[64,16,4,1]{3,2,1,0:T(4,128)(2,1)} %get-tuple-element.83) | data formatting | bytes 16384 | tf_op jit(solution)/shard_map/squeeze | solution.py:31
  34.9 7.9 %copy.136 = bf16[64,16,4,1]{2,0,1,3:T(8,128)(2,1)} copy(bf16[64,16,4,1]{3,2,1,0:T(4,128)(2,1)} %get-tuple-element.82) | data formatting | bytes 16384 | tf_op jit(solution)/shard_map/squeeze | solution.py:32
  44.9 3.3 %concatenate.50 = bf16[64,16,268]{2,0,1:T(8,128)(2,1)S(1)} concatenate(bf16[64,16,128]{2,0,1:T(8,128)(2,1)} %get-tuple-element.92, bf16[64,16,128]{2,0,1:T(8,128)(2,1)} %get-tuple-element.91, bf16[64,16,4]{2,0,1:T(8,128)(2,1)} %bitcast.220, bf16[64,16,4]{2,0,1:T(8,128)(2,1)} %bitcast.221, bf16[64,16,1]{2,0,1:T(8,128)(2,1)} %copy.73, bf16[64,16,1]{2,0,1:T(8,128)(2,1)} %copy.74, ...), dimensions={2} | concatenate | bytes 1097728 | tf_op jit(solution)/shard_map/concatenate | solution.py:27
  48.3 5.8 %collective-permute-start = (bf16[64,16,268]{2,0,1:T(8,128)(2,1)S(1)}, bf16[64,16,268]{2,0,1:T(8,128)(2,1)}, u32[]{:S(2)}, u32[]{:S(2)}) collective-permute-start(bf16[64,16,268]{2,0,1:T(8,128)(2,1)S(1)} %concatenate.50), channel_id=1, source_target_pairs={{0,4},{4,8},{8,12},{1,5},{5,9},{9,13},{2,6},{6,10},{10,14},{3,7},{... | collective-permute-start | bytes 1646600 | tf_op jit(solution)/shard_map/ppermute | solution.py:17
  57.5 12.5 %collective-permute-done = bf16[64,16,268]{2,0,1:T(8,128)(2,1)} collective-permute-done((bf16[64,16,268]{2,0,1:T(8,128)(2,1)S(1)}, bf16[64,16,268]{2,0,1:T(8,128)(2,1)}, u32[]{:S(2)}, u32[]{:S(2)}) %collective-permute-start) | collective-permute-done | bytes 548896 | tf_op jit(solution)/shard_map/ppermute | solution.py:17
  70.0 5.1 %collective-permute-done.1 = bf16[64,16,268]{2,0,1:T(8,128)(2,1)} collective-permute-done((bf16[64,16,268]{2,0,1:T(8,128)(2,1)S(1)}, bf16[64,16,268]{2,0,1:T(8,128)(2,1)}, u32[]{:S(2)}, u32[]{:S(2)}) %collective-permute-start.1) | collective-permute-done | bytes 548896 | tf_op jit(solution)/shard_map/ppermute | solution.py:19
  78.4 5.8 %gather_fusion = bf16[128,64,268]{2,1,0:T(8,128)(2,1)} fusion(bf16[64,48,268]{2,0,1:T(8,128)(2,1)} %pad_maximum_fusion.1, s32[1024]{0:T(1024)S(1)} %pad_clamp_fusion), kind=kCustom, calls=%fused_computation | custom fusion | bytes 8782336 | tf_op jit(solution)/shard_map/jit(_take)/gather | solution.py:45
  84.1 13.8 %copy.78 = bf16[64,16,8,268]{0,1,3,2:T(8,128)(2,1)} copy(bf16[64,16,8,268]{3,0,2,1:T(8,128)(2,1)} %bitcast.213) | data formatting | bytes 8781824 | tf_op jit(solution)/shard_map/jit(_take)/gather | solution.py:45
  97.9 7.9 %select_select_fusion = bf16[64,16,8,268]{0,1,3,2:T(8,128)(2,1)} fusion(bf16[64,16,8,268]{0,1,3,2:T(8,128)(2,1)} %copy.78, pred[16,8]{0,1:T(8,128)(4,1)S(1)} %get-tuple-element.65, pred[16,8]{0,1:T(8,128)(4,1)S(1)} %get-tuple-element.88), kind=kLoop, calls=%fused_computation.10 | loop fusion | flops 4390912 | bytes 8782080 | tf_op jit(solution)/shard_map/jit(_where)/select_n | solution.py:48
  121.5 4.2 %pad_maximum_fusion = bf16[64,4,4,6,130]{4,0,3,2,1:T(8,128)(2,1)} fusion(bf16[64,4,4,1,130]{4,0,3,2,1:T(8,128)(2,1)S(1)} %maximum_bitcast_fusion.1, bf16[64,4,4,4,1]{4,0,3,2,1:T(8,128)(2,1)} %copy.84, bf16[64,4,4,4,128]{4,0,3,2,1:T(8,128)(2,1)S(1)} %bitcast.216, bf16[64,4,4,4,1]{4,0,3,2,1:T(8,128)(2,1)} %copy.83, ...), kind=kLoop, calls=%fused_computation.36 | loop fusion | flops 7987200 | bytes 3194880 | tf_op jit(solution)/shard_map/concatenate | solution.py:71
  125.8 4.8 %all-to-all-start = ((bf16[64,4,4,6,130]{4,0,3,2,1:T(8,128)(2,1)}), bf16[64,4,4,6,130]{4,0,3,2,1:T(8,128)(2,1)}, u32[]{:S(2)}, u32[]{:S(2)}) async-start(bf16[64,4,4,6,130]{4,0,3,2,1:T(8,128)(2,1)} %pad_maximum_fusion), calls=%async_computation | async-start | bytes 6291456 | tf_op jit(solution)/shard_map/all_to_all | solution.py:138
  133.7 35.2 %all-reduce.2 = (bf16[256]{0:T(256)(128)(2,1)S(1)}, bf16[256]{0:T(256)(128)(2,1)S(1)}) all-reduce(bf16[256]{0:T(256)(128)(2,1)S(1)} %dynamic-update-slice, bf16[256]{0:T(256)(128)(2,1)S(1)} %dynamic-update-slice.1), channel_id=1, replica_groups=mesh['ens'=2,'tile'=4,'chan'=2,'sec'=2] {'chan','sec'}, use_global_device_ids=true, to_apply=%add | all-reduce | flops 512 | bytes 2048
  169.0 5.1 %all-gather = bf16[4,1,256]{2,1,0:T(2,128)(2,1)S(1)} all-gather(bf16[1,1,256]{2,1,0:T(2,128)(2,1)S(1)} %reshape.158), channel_id=1, replica_groups=mesh['ens'=2,'tile'=4,'chan'=2,'sec'=2] {'chan','sec'}, dimensions={0}, use_global_device_ids=true | all-gather | bytes 2560 | tf_op jit(solution)/shard_map/all_gather | solution.py:131
  174.1 7.3 %all_gather.25 = bf16[256,1024]{1,0:T(8,128)(2,1)S(1)} all-gather(bf16[256,256]{1,0:T(8,128)(2,1)S(1)} %copy-done.9), channel_id=1, replica_groups=mesh['ens'=2,'tile'=4,'chan'=2,'sec'=2] {'chan','sec'}, dimensions={1}, use_global_device_ids=true | all-gather | bytes 655360 | tf_op jit(solution)/shard_map/all_gather | solution.py:130
  181.4 7.9 %all_gather.21 = bf16[1024,256]{1,0:T(8,128)(2,1)} all-gather(bf16[256,256]{1,0:T(8,128)(2,1)S(1)} %copy-done.10), channel_id=1, replica_groups=mesh['ens'=2,'tile'=4,'chan'=2,'sec'=2] {'chan','sec'}, dimensions={0}, use_global_device_ids=true | all-gather | bytes 655360 | tf_op jit(solution)/shard_map/all_gather | solution.py:132
  189.4 7.3 %copy.90 = bf16[4,64,1,4,6,130]{1,0,5,4,3,2:T(4,128)(2,1)} copy(bf16[4,64,1,4,6,130]{5,1,4,3,0,2:T(8,128)(2,1)} %bitcast.24) | data formatting | bytes 3194880 | tf_op jit(solution)/shard_map/all_to_all | solution.py:138
  196.7 5.1 %squeeze.76 = bf16[256,4,6,130]{0,3,2,1:T(8,128)(2,1)} reshape(bf16[4,64,1,4,6,130]{1,0,5,4,3,2:T(4,128)(2,1)} %copy.90) | data formatting | bytes 3194880 | tf_op jit(solution)/shard_map/squeeze | solution.py:138
  209.5 20.8 %fusion.7 = bf16[1024,4,4,128]{0,3,2,1:T(8,128)(2,1)} fusion(f32[1024]{0:T(1024)S(1)} %bitcast.234, f32[4,4,128,256]{3,2,1,0:T(8,128)S(1)} %get-tuple-element.90, f32[256]{0:T(256)S(1)} %convert_element_type.43, f32[4,4,128]{2,1,0:T(4,128)S(1)} %add_rsqrt_fusion, bf16[256,1024]{1,0:T(8,128)(2,1)S(1)} %all_gather.25), kind=kOutput, calls=%fused_computation.13 | convolution fusion | flops 1213726720 | bytes 6829056 | tf_op jit(solution)/shard_map/csij,ch->hsij/dot_general | solution.py:149
  230.3 7.9 %reshape.134 = bf16[4,256,4,4,128]{1,0,4,3,2:T(4,128)(2,1)} reshape(bf16[1024,4,4,128]{0,3,2,1:T(8,128)(2,1)} %fusion.7) | data formatting | bytes 8388608 | tf_op jit(solution)/shard_map/reshape | solution.py:153
  238.2 7.5 %copy.101 = bf16[4,256,4,4,128]{4,1,3,2,0:T(8,128)(2,1)} copy(bf16[4,256,4,4,128]{1,0,4,3,2:T(4,128)(2,1)} %reshape.134) | data formatting | bytes 8388608
  245.7 9.9 %while.11 = (s32[]{:T(128)}, f32[256,4,4,128]{3,0,2,1:T(8,128)S(1)}, bf16[4,256,256]{2,1,0:T(8,128)(2,1)}, bf16[4,256,4,4,128]{4,1,3,2,0:T(8,128)(2,1)}, s32[]{:T(128)}, /*index=5*/s32[]{:T(128)}) while((s32[]{:T(128)}, f32[256,4,4,128]{3,0,2,1:T(8,128)S(1)}, bf16[4,256,256]{2,1,0:T(8,128)(2,1)}, ...), condition=%wide.region_2.3_spmd.clone, body=%wide.region_1.2_spmd.clone.sunk | while | flops 270532608 | bytes 7472207 | solution.py:154
  262.8 29.4 %gather_fusion.1 = bf16[8192,64]{1,0:T(8,128)(2,1)} fusion(bf16[64,8192]{0,1:T(8,128)(2,1)S(1)} %copy.103, s32[8192]{0:T(1024)S(1)} %broadcast_clamp_fusion), kind=kCustom, calls=%fused_computation.1 | custom fusion | bytes 2129920 | tf_op jit(solution)/shard_map/jit(_take)/gather | solution.py:124
  (134 shorter events, 76.6 us)
Async XLA Ops:
  6.5 124.1 %copy-start = (bf16[2048,384]{1,0:T(8,128)(2,1)S(1)}, bf16[2048,384]{1,0:T(8,128)(2,1)}, u32[]{:S(2)}) copy-start(bf16[2048,384]{1,0:T(8,128)(2,1)} %param.16) | copy-start | bytes 4718596
  6.5 9.3 %copy-start.3 = (bf16[64,16,4,128]{3,2,1,0:T(4,128)(2,1)S(1)}, bf16[64,16,4,128]{3,2,1,0:T(4,128)(2,1)}, u32[]{:S(2)}) copy-start(bf16[64,16,4,128]{3,2,1,0:T(4,128)(2,1)} %param.15) | copy-start | bytes 3145732
  6.5 195.2 %all-gather.4.cloned.1.call-start = ((), (), s32[]{:S(2)}) async-start(), calls=%async_computation.1 | async-start | bytes 1474560 | tf_op jit(solution)/shard_map/all_gather | solution.py:127
  34.9 22.4 %copy-start.14 = (s32[16,8]{0,1:T(8,128)S(1)}, s32[16,8]{0,1:T(8,128)}, u32[]{:S(2)}) copy-start(s32[16,8]{0,1:T(8,128)} %param.26) | copy-start | bytes 1540
  48.3 21.7 %collective-permute-start = (bf16[64,16,268]{2,0,1:T(8,128)(2,1)S(1)}, bf16[64,16,268]{2,0,1:T(8,128)(2,1)}, u32[]{:S(2)}, u32[]{:S(2)}) collective-permute-start(bf16[64,16,268]{2,0,1:T(8,128)(2,1)S(1)} %concatenate.50), channel_id=1, source_target_pairs={{0,4},{4,8},{8,12},{1,5},{5,9},{9,13},{2,6},{6,10},{10,14},{3,7},{... | collective-permute-start | bytes 1646600 | tf_op jit(solution)/shard_map/ppermute | solution.py:17
  54.1 21.0 %collective-permute-start.1 = (bf16[64,16,268]{2,0,1:T(8,128)(2,1)S(1)}, bf16[64,16,268]{2,0,1:T(8,128)(2,1)}, u32[]{:S(2)}, u32[]{:S(2)}) collective-permute-start(bf16[64,16,268]{2,0,1:T(8,128)(2,1)S(1)} %concatenate.50), channel_id=1, source_target_pairs={{4,0},{8,4},{12,8},{5,1},{9,5},{13,9},{6,2},{10,6},{14,10},{7,3},{... | collective-permute-start | bytes 1646600 | tf_op jit(solution)/shard_map/ppermute | solution.py:19
  108.4 13.1 %copy-start.7 = (bf16[64,16,4,128]{3,0,2,1:T(8,128)(2,1)S(1)}, bf16[64,16,4,128]{3,0,2,1:T(8,128)(2,1)}, u32[]{:S(2)}) copy-start(bf16[64,16,4,128]{3,0,2,1:T(8,128)(2,1)} %copy.82) | copy-start | bytes 3145732
  125.7 4.9 %copy-start.12 = (bf16[384,64]{0,1:T(8,128)(2,1)S(1)}, bf16[384,64]{0,1:T(8,128)(2,1)}, u32[]{:S(2)}) copy-start(bf16[384,64]{0,1:T(8,128)(2,1)} %param.17) | copy-start | bytes 147460
  125.7 6.3 %copy-start.19 = (u32[32]{0:T(128)S(1)}, u32[32]{0:T(128)}, u32[]{:S(2)}) copy-start(u32[32]{0:T(128)} %constant.178) | copy-start | bytes 388
  125.7 7.5 %copy-start.15 = (bf16[64]{0:T(256)(128)(2,1)S(1)}, bf16[64]{0:T(256)(128)(2,1)}, u32[]{:S(2)}) copy-start(bf16[64]{0:T(256)(128)(2,1)} %param.19) | copy-start | bytes 388
  125.7 7.8 %copy-start.16 = (bf16[64]{0:T(256)(128)(2,1)S(1)}, bf16[64]{0:T(256)(128)(2,1)}, u32[]{:S(2)}) copy-start(bf16[64]{0:T(256)(128)(2,1)} %param.20) | copy-start | bytes 388
  125.7 43.3 %copy-start.17 = (bf16[256]{0:T(256)(128)(2,1)S(1)}, bf16[256]{0:T(256)(128)(2,1)}, u32[]{:S(2)}) copy-start(bf16[256]{0:T(256)(128)(2,1)} %param.22) | copy-start | bytes 1540
  125.7 48.4 %copy-start.9 = (bf16[256,256]{1,0:T(8,128)(2,1)S(1)}, bf16[256,256]{1,0:T(8,128)(2,1)}, u32[]{:S(2)}) copy-start(bf16[256,256]{1,0:T(8,128)(2,1)} %param.21) | copy-start | bytes 393220
  125.7 55.7 %copy-start.10 = (bf16[256,256]{1,0:T(8,128)(2,1)S(1)}, bf16[256,256]{1,0:T(8,128)(2,1)}, u32[]{:S(2)}) copy-start(bf16[256,256]{1,0:T(8,128)(2,1)} %param.23) | copy-start | bytes 393220
  125.8 63.6 %copy-start.11 = (s32[16,4,128]{2,1,0:T(4,128)S(1)}, s32[16,4,128]{2,1,0:T(4,128)}, u32[]{:S(2)}) copy-start(s32[16,4,128]{2,1,0:T(4,128)} %param.27) | copy-start | bytes 98308
  125.8 63.6 %all-to-all-start = ((bf16[64,4,4,6,130]{4,0,3,2,1:T(8,128)(2,1)}), bf16[64,4,4,6,130]{4,0,3,2,1:T(8,128)(2,1)}, u32[]{:S(2)}, u32[]{:S(2)}) async-start(bf16[64,4,4,6,130]{4,0,3,2,1:T(8,128)(2,1)} %pad_maximum_fusion), calls=%async_computation | async-start | bytes 6291456 | tf_op jit(solution)/shard_map/all_to_all | solution.py:138
  130.5 130.2 %all-gather.6.cloned.1.call-start = ((), (), s32[]{:S(2)}) async-start(), calls=%async_computation.2 | async-start | bytes 1310720 | tf_op jit(solution)/shard_map/all_gather | solution.py:122
  255.5 5.1 %copy-start.13 = (s32[16,4,128]{2,1,0:T(4,128)S(1)}, s32[16,4,128]{2,1,0:T(4,128)}, u32[]{:S(2)}) copy-start(s32[16,4,128]{2,1,0:T(4,128)} %param.25) | copy-start | bytes 98308
  255.6 5.1 %copy-start.18 = (bf16[64]{0:T(256)(128)(2,1)S(1)}, bf16[64]{0:T(256)(128)(2,1)}, u32[]{:S(2)}) copy-start(bf16[64]{0:T(256)(128)(2,1)} %param.24) | copy-start | bytes 388
  258.5 37.0 %collective-permute-start.2 = (f32[64,1,4,4,128]{4,0,3,2,1:T(8,128)}, f32[64,1,4,4,128]{4,0,3,2,1:T(8,128)}, u32[]{:S(2)}, u32[]{:S(2)}) collective-permute-start(f32[64,1,4,4,128]{4,0,3,2,1:T(8,128)} %get-tuple-element.77), channel_id=1, source_target_pairs={{0,3},{1,0},{2,1},{3,2},{4,7},{5,4},{6,5},{7,6},{8,11},{9,8},{10,9... | collective-permute-start | bytes 1572872 | tf_op jit(solution)/shard_map/ppermute | solution.py:165
  260.1 36.5 %collective-permute-start.3 = (f32[64,1,4,4,128]{4,0,3,2,1:T(8,128)}, f32[64,1,4,4,128]{4,0,3,2,1:T(8,128)}, u32[]{:S(2)}, u32[]{:S(2)}) collective-permute-start(f32[64,1,4,4,128]{4,0,3,2,1:T(8,128)} %get-tuple-element.76), channel_id=1, source_target_pairs={{0,2},{1,3},{2,0},{3,1},{4,6},{5,7},{6,4},{7,5},{8,10},{9,11},{10,... | collective-permute-start | bytes 1572872 | tf_op jit(solution)/shard_map/ppermute | solution.py:165
  260.6 37.1 %collective-permute-start.4 = (f32[64,1,4,4,128]{4,0,3,2,1:T(8,128)}, f32[64,1,4,4,128]{4,0,3,2,1:T(8,128)}, u32[]{:S(2)}, u32[]{:S(2)}) collective-permute-start(f32[64,1,4,4,128]{4,0,3,2,1:T(8,128)} %get-tuple-element.75), channel_id=1, source_target_pairs={{0,1},{1,2},{2,3},{3,0},{4,5},{5,6},{6,7},{7,4},{8,9},{9,10},{10,1... | collective-permute-start | bytes 1572872 | tf_op jit(solution)/shard_map/ppermute | solution.py:165
  292.2 6.6 %copy-start.6 = (f32[256,1,4,4,128]{4,0,3,2,1:T(8,128)S(1)}, f32[256,1,4,4,128]{4,0,3,2,1:T(8,128)}, u32[]{:S(2)}) copy-start(f32[256,1,4,4,128]{4,0,3,2,1:T(8,128)} %copy-done.5) | copy-start | bytes 6291460
  302.2 4.0 %copy-start.1 = (bf16[2048,384]{1,0:T(8,128)(2,1)S(1)}, bf16[2048,384]{1,0:T(8,128)(2,1)}, u32[]{:S(2)}) copy-start(bf16[2048,384]{1,0:T(8,128)(2,1)} %param.16) | copy-start | bytes 4718596
  (4 other events, 10.2 us)
Sparse Core Ops, SparseCore 0:
  55.7 19.6 all-gather.3
  133.0 27.7 all-gather.5
